TPU v7x, 512 devices: a whole 4x8x8 slice. The times are simulated.
512 devices in a mesh: fine: 128 (over z_hi, y, x, core), sub: 4 (over z_lo).
Axes of the slice: x: 4, y: 8, z: 8 (z_hi: 2, z_lo: 4; z = z_hi * 4 + z_lo), core: 2. Of those that a mesh axis runs over, the one named last changes fastest.
Arguments:
- rhs: float32 [1024, 128, 128], P('fine', 'sub'), may hold values from -6 to 6
- density: float32 [1024, 128, 128], P('fine', 'sub'), may hold values from 0.2 to 5
Outputs:
- solution: float32 [1024, 128, 128], P('fine', 'sub')
- residual: float32 [1024, 128, 128], P('fine', 'sub')
All inputs are finite; a program needn't handle non-finite values.
Results may differ from a plain program's by a relative error of at most 0.00014.
Values sent between devices are 32-bit elements; how exact they have to be, the bound alone decides.
A program may use at most 64 MiB of HBM per device.

v0:
```python
import functools

import jax
import jax.numpy as jnp
from jax import lax
from jax.experimental import pallas as pl
from jax.experimental.pallas import tpu as pltpu
from jax.sharding import PartitionSpec as P

DEGREE = 4
CYCLES = 2
MESH = pl.DeviceIdType.MESH
F32 = jnp.float32
BF16 = jnp.bfloat16
ROW = 8
PLANES = (8, 4, 2)
ROWS = (32, 16, 8)


def chebyshev_constants(lower):
    upper = 2.0
    theta = 0.5 * (upper + lower)
    delta = 0.5 * (upper - lower)
    sigma = theta / delta
    ratio = 1.0 / sigma
    steps = []
    for _ in range(DEGREE - 1):
        next_ratio = 1.0 / (2.0 * sigma - ratio)
        steps.append((next_ratio * ratio, 2.0 * next_ratio / delta))
        ratio = next_ratio
    return 1.0 / theta, steps


def iota(shape, dim):
    return lax.broadcasted_iota(jnp.int32, shape, dim)


def roll(value, shift, axis):
    return pltpu.roll(value, shift % value.shape[axis], axis)


def invert(value):
    return pltpu.reciprocal(value, full_range=False)


def one_hot(condition):
    return jnp.where(condition, 1.0, 0.0).astype(F32)


def one_hot_matmul(value, matrix):
    count = value.shape[0]
    first = value.astype(BF16).astype(F32)
    rest = value - first
    second = rest.astype(BF16).astype(F32)
    parts = jnp.concatenate([first, second, rest - second], axis=0).astype(BF16)
    product = jnp.dot(parts, matrix, preferred_element_type=F32)
    return product[0:count] + product[count : 2 * count] + product[2 * count :]


def restrict_block(source, first, planes, rows, stride, work):
    field = source[first : first + planes, 0:rows, :]
    field = field.reshape(planes // 2, 2, rows, 128)
    work[0 : planes // 2, 0:rows, :] = field[:, 0] + field[:, 1]
    half = rows // 2
    both = (
        work[0 : planes // 2, pl.ds(0, half, stride=2), :]
        + work[0 : planes // 2, pl.ds(1, half, stride=2), :]
    )
    lane = iota(both.shape, 2)
    even = (lane // stride) % 2 == 0
    other = jnp.where(even, roll(both, -stride, 2), roll(both, stride, 2))
    return (both + other) * 0.125


def fine_coefficients(level, dens, coef, low, high):
    own = ROWS[level]
    scale = 2.0 * 0.25**level
    stride = 2**level
    face_z, face_x, face_y, diagonal, inverse = coef
    shape = (own + 16, 128)

    def compress(value):
        tail = jnp.where(
            iota((8, 128), 0) < 4, value[own : own + 8], value[own + 8 : own + 16]
        )
        return jnp.concatenate([value[0:own], tail], axis=0)

    def plane(p, down):
        here = dens[p + 1]
        above = dens[p + 2]
        lane = iota(shape, 1)
        right = roll(here, -1, 0)
        up = scale * invert(jnp.maximum(here + above, 0.1))
        x_face = scale * invert(jnp.maximum(here + right, 0.1))
        ahead = jnp.where(lane >= 128 - stride, 0.0, roll(here, -stride, 1))
        behind = jnp.where(lane < stride, 0.0, roll(here, stride, 1))
        y_face = scale * invert(jnp.maximum(here + ahead, 0.1))
        y_back = scale * invert(jnp.maximum(here + behind, 0.1))
        diag = up + down + x_face + roll(x_face, 1, 0) + y_face + y_back
        inside = here > 0.0
        face_z[p] = compress(jnp.where(inside & (above > 0.0), up, 0.0))
        face_x[p] = compress(jnp.where(inside & (right > 0.0), x_face, 0.0))
        face_y[p] = compress(jnp.where(lane >= 128 - stride, 0.0, y_face))
        diagonal[p] = compress(diag)
        inverse[p] = compress(invert(diag))
        return up

    lowest = scale * invert(jnp.maximum(dens[low] + dens[low + 1], 0.1))
    lax.fori_loop(low, high, plane, lowest, unroll=True)


def fine_apply(field, p, coef, q, stride):
    face_z, face_x, face_y, diagonal, _ = coef
    here = field[p]
    x_face = face_x[q]
    y_face = face_y[q]
    result = diagonal[q] * here
    result = result - face_z[q] * field[p + 1] - face_z[q - 1] * field[p - 1]
    result = result - x_face * roll(here, -1, 0) - roll(x_face * here, 1, 0)
    result = result - y_face * roll(here, -stride, 1) - roll(y_face * here, stride, 1)
    return result


def fine_smooth(level, source, coef, remain, updates, answer):
    planes = PLANES[level] + 8
    stride = 2**level
    inverse = coef[4]
    first, steps = chebyshev_constants(0.5)
    d0, d1, d2 = updates

    def start(p, carry):
        d0[p] = source[p] * inverse[p] * first
        return carry

    lax.fori_loop(0, planes, start, 0, unroll=True)
    chain = (d0, d1, d2)
    for sweep in range(3):
        old = chain[sweep]
        keep, add = steps[sweep]

        def step(p, carry, sweep=sweep, old=old, keep=keep, add=add):
            left = source[p] if sweep == 0 else remain[p]
            left = left - fine_apply(old, p, coef, p, stride)
            new = keep * old[p] + add * (left * inverse[p])
            if sweep < 2:
                remain[p] = left
                chain[sweep + 1][p] = new
            else:
                answer[p] = d0[p] + d1[p] + d2[p] + new
            return carry

        lax.fori_loop(sweep + 1, planes - sweep - 1, step, 0, unroll=True)


def packed_coefficients(dens, ny, nx, scale):
    rows = dens.shape[0]
    z = iota(dens.shape, 0)
    lane = iota(dens.shape, 1)
    y = lane % ny
    x = lane // ny
    scale = 2.0 * scale

    def neighbour(shift, axis, outside):
        return jnp.where(outside, 0.0, roll(dens, shift, axis))

    above = neighbour(-1, 0, z == rows - 1)
    below = neighbour(1, 0, z == 0)
    right = neighbour(-ny, 1, x >= nx - 1)
    left = neighbour(ny, 1, x == 0)
    ahead = neighbour(-1, 1, y == ny - 1)
    behind = neighbour(1, 1, y == 0)

    def face(other):
        return scale * invert(jnp.maximum(dens + other, 0.1))

    up, x_face, y_face = face(above), face(right), face(ahead)
    diagonal = up + face(below) + x_face + face(left) + y_face + face(behind)
    inside = dens > 0.0

    def inner(value, other):
        return jnp.where(inside & (other > 0.0), value, 0.0)

    return (
        inner(up, above),
        inner(x_face, right),
        inner(y_face, ahead),
        jnp.where(inside, diagonal, 0.0),
        jnp.where(inside, invert(diagonal), 0.0),
    )


def packed_apply(field, coef, ny):
    face_z, face_x, face_y, diagonal, _ = coef
    result = diagonal * field
    result = result - face_z * roll(field, -1, 0) - roll(face_z * field, 1, 0)
    result = result - face_x * roll(field, -ny, 1) - roll(face_x * field, ny, 1)
    result = result - face_y * roll(field, -1, 1) - roll(face_y * field, 1, 1)
    return result


def packed_smooth(source, coef, ny, lower):
    first, steps = chebyshev_constants(lower)
    inverse = coef[4]
    update = source * inverse * first
    answer = update
    for keep, add in steps:
        source = source - packed_apply(update, coef, ny)
        update = keep * update + add * (source * inverse)
        answer = answer + update
    return answer


PIECES = {
    ("a", 1): ((("D1", 5, 1, 4), ("D2", 5, 3, 2)), (("R1", 4, 0, 4), ("R2", 4, 2, 2))),
    ("a", -1): ((("D1", 5, 9, 4), ("D2", 5, 7, 2)), (("R1", 4, 8, 4), ("R2", 4, 6, 2))),
    ("a", 2): ((("D1", 8, 0, 1), ("D2", 5, 1, 2)), (("R2", 4, 0, 2),)),
    ("a", -2): ((("D1", 5, 13, 1), ("D2", 5, 9, 2)), (("R2", 4, 8, 2),)),
    ("a", 3): ((("D2", 6, 0, 1),), ()),
    ("a", -3): ((("D2", 5, 11, 1),), ()),
    ("b", 1): (
        (("D0", 9, 1, 4), ("D1", 5, 1, 4), ("D2", 5, 3, 2)),
        (("R0", 9, 1, 3), ("R1", 4, 0, 4), ("R2", 4, 2, 2)),
    ),
    ("b", -1): (
        (("D0", 5, 13, 4), ("D1", 5, 9, 4), ("D2", 5, 7, 2)),
        (("R0", 4, 12, 3), ("R1", 4, 8, 4), ("R2", 4, 6, 2)),
    ),
    ("b", 2): ((("D2", 5, 1, 2),), (("R2", 4, 0, 2),)),
    ("b", -2): ((("D2", 5, 9, 2),), (("R2", 4, 8, 2),)),
}
WHOLE = (("D0", 1, 3, 0, 5), ("D0", -1, 0, 13, 5), ("R0", 1, 4, 0, 4), ("R0", -1, 0, 12, 4))


def whole_messages(with_density):
    return WHOLE if with_density else WHOLE[2:]


def z_messages(with_density):
    result = []
    for (part, shift), (density, field) in PIECES.items():
        pieces = (density if with_density else ()) + field
        if pieces:
            result.append((part, shift, pieces))
    return result


def paired(name, tiles):
    return name[1] != "0" and tiles % 2 == 0


def piece_tiles(part, piece):
    name, _, _, count = piece
    tiles = count * (ROWS[int(name[1])] // 8 if part == "a" else 1)
    return tiles // 2 if paired(name, tiles) else tiles


def x_pieces(with_density):
    result = []
    for level in range(3):
        count = PLANES[level]
        if with_density:
            result.append(("D%d" % level, count, count // 2 if level else count))
        result.append(("R%d" % level, count, (4, 1, 1)[level]))
    return result


def buffer_shapes(with_density):
    tiles = [sum(sent for _, _, sent in x_pieces(with_density))] * 2
    for part, _, pieces in z_messages(with_density):
        tiles.append(sum(piece_tiles(part, piece) for piece in pieces))
    return [pltpu.VMEM((count, 8, 128), F32) for count in tiles]


def whole_shapes(with_density):
    return [pltpu.VMEM((count, 32, 128), F32) for _, _, _, _, count in whole_messages(with_density)]


def n_halo(with_density):
    return 2 + len(z_messages(with_density))


def even_lanes(tiles):
    return iota((tiles, 8, 128), 2) % 2 == 0


def upper_rows(tiles):
    return iota((tiles, 8, 128), 1) < 4


def pack_lanes(block):
    half = block.shape[0] // 2
    return jnp.where(even_lanes(half), block[0:half], block[half:])


def unpack_lanes(block):
    even = even_lanes(block.shape[0])
    return jnp.concatenate(
        [jnp.where(even, block, roll(block, 1, 2)), jnp.where(even, roll(block, -1, 2), block)],
        axis=0,
    )


def partners_of(place):
    k, s, _, ns = place
    i, y, half = k % ROW, k // ROW % 8, k // (8 * ROW)
    depth, side = [], []
    for delta in (4, 3, 5, 2, 6, 1, 7):
        z = (half * ns + s + delta) % (2 * ns)
        depth.append((((z // ns) * 8 + y) * ROW + i, z % ns))
        side.append((delta, ((half * 8 + (y + delta) % 8) * ROW + i, s)))
    return depth, side


class Phase:
    def __init__(self, refs, place, with_density, buffers, coarse, send_sem, recv_sem):
        send, recv, whole = buffers
        self.whole_in = whole
        self.whole = whole_messages(with_density)
        self.refs = refs
        self.k, self.s, self.nf, self.ns = place
        self.dense = with_density
        self.send, self.recv = send, recv
        self.row, self.row_in, self.depth_in, self.side_in = coarse
        self.send_sem, self.recv_sem = send_sem, recv_sem
        self.started = []
        self.count = 0
        self.z = z_messages(with_density)
        self.copies = {}
        self.i = self.k % ROW
        self.g = self.k // ROW
        self.ng = self.nf // ROW
        self.y = self.g % 8
        self.z_at = self.g // 8 * self.ns + self.s
        self.depth_partners, self.side_partners = partners_of(place)

    def start(self, source, target, k, s, shift=0):
        index = self.count
        self.count += 1
        copy = pltpu.make_async_remote_copy(
            src_ref=source,
            dst_ref=target,
            send_sem=self.send_sem.at[index],
            recv_sem=self.recv_sem.at[index],
            device_id=(k, s),
            device_id_type=MESH,
        )
        self.when(self.has_target(shift), copy.start)
        self.started.append((copy, shift))
        return copy

    def has_target(self, shift):
        if shift == 0:
            return None
        return self.k < self.nf - shift if shift > 0 else self.k >= -shift

    def has_source(self, shift):
        return self.has_target(-shift)

    def when(self, condition, action):
        if condition is None:
            action()
        else:
            pl.when(condition)(action)

    def start_whole(self, fields):
        self.whole_copies = []
        for index, (name, shift, first, _, count) in enumerate(self.whole):
            target = (self.k + shift + self.nf) % self.nf
            ref, lead = fields[name]
            source = ref.at[lead + first : lead + first + count, 0:32, :]
            self.whole_copies.append(
                self.start(source, self.whole_in[index], target, self.s, shift)
            )

    def unpack_whole(self):
        for index, (name, shift, _, target, count) in enumerate(self.whole):
            self.when(self.has_source(shift), self.whole_copies[index].wait_recv)
        for index, (name, shift, _, target, count) in enumerate(self.whole):
            block = jnp.where(self.has_source(shift), self.whole_in[index][...], 0.0)
            self.refs[name][target : target + count, 0:32, :] = block

    def pack_x(self):
        for which in (0, 1):
            at = 0
            for name, count, sent in x_pieces(self.dense):
                level = int(name[1])
                lead = 5 if name[0] == "D" else 4
                row = ROWS[level] - 8 if which == 0 else 0
                block = self.refs[name][lead : lead + count, row : row + 8, :]
                if level:
                    block = pack_lanes(block)
                if block.shape[0] > sent:
                    near, far = block[0:sent], roll(block[sent:], 4, 1)
                    upper = upper_rows(sent)
                    if which == 0:
                        block = jnp.where(upper, far, near)
                    else:
                        block = jnp.where(upper, near, far)
                self.send[which][at : at + sent] = block
                at += sent

    def start_x(self):
        up, down = (self.s + 1) % self.ns, (self.s + self.ns - 1) % self.ns
        self.x_copies = [
            self.start(self.send[0], self.recv[0], self.k, up),
            self.start(self.send[1], self.recv[1], self.k, down),
        ]

    def unpack_x(self):
        for copy in self.x_copies:
            copy.wait_recv()
        low_in = jnp.where(self.s > 0, 1.0, 0.0).astype(F32)
        high_in = jnp.where(self.s < self.ns - 1, 1.0, 0.0).astype(F32)
        at = 0
        for name, count, sent in x_pieces(self.dense):
            level = int(name[1])
            own = ROWS[level]
            lead = 5 if name[0] == "D" else 4
            low, high = self.recv[0][at : at + sent], self.recv[1][at : at + sent]
            at += sent
            ref = self.refs[name]
            if name[0] == "D":
                if level:
                    low, high = unpack_lanes(low), unpack_lanes(high)
                ref[lead : lead + count, own : own + 8, :] = high * high_in
                ref[lead : lead + count, own + 8 : own + 16, :] = low * low_in
                continue
            upper = upper_rows(sent)
            block = jnp.where(upper, high, low)
            if sent < (count // 2 if level else count):
                far = roll(jnp.where(upper, low, high), 4, 1)
                block = jnp.concatenate([block, far], axis=0)
            if level:
                block = unpack_lanes(block)
            ref[lead : lead + count, own : own + 8, :] = block

    def pack_z(self, part):
        for index, (kind, _, pieces) in enumerate(self.z):
            if kind != part:
                continue
            at = 0
            for piece in pieces:
                name, source, _, count = piece
                ref, own = self.refs[name], ROWS[int(name[1])]
                if part == "a":
                    block = ref[source : source + count, 0:own, :]
                    block = block.reshape(count * own // 8, 8, 128)
                else:
                    block = ref[source : source + count, own : own + 8, :]
                    if name[0] == "D":
                        low = ref[source : source + count, own + 8 : own + 16, :]
                        block = jnp.where(upper_rows(count), block, low)
                if paired(name, block.shape[0]):
                    block = pack_lanes(block)
                self.send[2 + index][at : at + block.shape[0]] = block
                at += block.shape[0]

    def start_z(self, part):
        for index, (kind, shift, _) in enumerate(self.z):
            if kind == part:
                target = (self.k + shift + self.nf) % self.nf
                self.copies[index] = self.start(
                    self.send[2 + index], self.recv[2 + index], target, self.s, shift
                )

    def unpack_z(self):
        for index, (_, shift, _) in enumerate(self.z):
            self.when(self.has_source(shift), self.copies[index].wait_recv)
        for index, (part, shift, pieces) in enumerate(self.z):
            inside = self.has_source(shift)
            at = 0
            for piece in pieces:
                name, _, target, count = piece
                ref, own = self.refs[name], ROWS[int(name[1])]
                sent = piece_tiles(part, piece)
                block = jnp.where(inside, self.recv[2 + index][at : at + sent], 0.0)
                at += sent
                if sent < (count * own // 8 if part == "a" else count):
                    block = unpack_lanes(block)
                if part == "a":
                    ref[target : target + count, 0:own, :] = block.reshape(count, own, 128)
                else:
                    ref[target : target + count, own : own + 8, :] = block
                    if name[0] == "D":
                        ref[target : target + count, own + 8 : own + 16, :] = block

    def pack_row(self, fields, pair, spread_row):
        for index, field in enumerate(fields):
            pillar = jnp.sum(field, axis=0).reshape(4, 8, 128)
            pair[4 * index : 4 * index + 4, :] = jnp.sum(pillar, axis=1) * 0.125**3
        spread = one_hot_matmul(pair[...], spread_row[...])[0:8]
        mine = iota((8, 128), 1) // 16 == iota((8, 128), 0)
        row = jnp.sum(jnp.where(mine, spread, 0.0), axis=0, keepdims=True)
        self.row[...] = row
        self.row_in[self.i] = row

    def start_rows(self):
        self.row_copies = []
        for delta in range(1, ROW):
            target = self.g * ROW + (self.i + delta) % ROW
            self.row_copies.append(
                self.start(self.row, self.row_in.at[self.i], target, self.s)
            )

    def start_depth(self):
        for copy in self.row_copies:
            copy.wait_recv()
        line = iota((8, 128), 0)
        tile = jnp.zeros((8, 128), F32)
        for index in range(ROW):
            tile = jnp.where(line == index, self.row_in[index], tile)
        self.depth_in[self.z_at] = tile
        self.depth_copies = []
        for k, s in self.depth_partners:
            slot = self.depth_in.at[self.z_at]
            self.depth_copies.append(self.start(slot, slot, k, s))

    def start_sides(self, work, pool):
        for copy in self.depth_copies:
            copy.wait_recv()
        left = iota((8, 128), 1) < 64
        slot = self.side_in.at[self.y]
        wide = []
        for half in range(2):
            tiles = [self.depth_in[4 * half + index] for index in range(4)]
            turned = [roll(tile, 64, 1) for tile in tiles]
            fields = [jnp.where(left, tiles[a], turned[a + 1]) for a in (0, 2)]
            if self.dense:
                fields += [jnp.where(left, turned[a], tiles[a + 1]) for a in (0, 2)]
            for index, field in enumerate(fields):
                slot[2 + len(fields) * half + index] = field
            wide.append(jnp.concatenate(fields, axis=1))
        wide = jnp.concatenate(wide, axis=0)
        sums = one_hot_matmul(wide, pool[0 : wide.shape[1], :])
        work[...] = sums[:, 0:128]
        line = iota((8, 128), 0)
        for half in range(2):
            four = work[pl.ds(8 * half, 4, stride=2), :] + work[pl.ds(8 * half + 1, 4, stride=2), :]
            slot[half, 0:4, :] = four * 0.125
            five = sums[8 * half : 8 * half + 8, 128:256]
            five = five + roll(five, -1, 0)
            five = (five + roll(five, -2, 0)) * (0.125 * 0.125)
            five = jnp.where(line % 2 == 0, five[0:1], five[4:5])
            slot[half, 4:8, :] = five[4:8]
        self.side_copies = []
        for delta, (k, s) in self.side_partners:
            if delta in (1, 7):
                self.side_copies.append(self.start(slot, slot, k, s))
            else:
                part = slot.at[0:2]
                self.side_copies.append(self.start(part, part, k, s))

    def wait_sides(self):
        for copy in self.side_copies:
            copy.wait_recv()

    def group_fields(self, group):
        wrapped = (group + self.ng) % self.ng
        y, half = wrapped % 8, wrapped // 8
        count = 4 if self.dense else 2
        tiles = [self.side_in[y, 2 + half * count + index] for index in range(count)]
        return [
            jnp.concatenate(tiles[at : at + 2], axis=1) for at in range(0, count, 2)
        ]

    def finish(self, first, last):
        for copy, shift in self.started[first:last]:
            self.when(self.has_target(shift), copy.wait_send)


def split_packed(value):
    left = iota(value.shape, 1) < 64
    return jnp.where(left, value, 0.0), jnp.where(left, roll(value, 64, 1), 0.0)


def build_matrices(pool, fan):
    line, lane = iota((128, 128), 0), iota((128, 128), 1)
    for half in range(4):
        x, y = line // 16 + 8 * (half % 2), line % 16
        rows = slice(128 * half, 128 * half + 128)
        home4 = (x // 2) * 8 + y // 2 + 64 * (half // 2)
        home5 = (x // 4) * 4 + y // 4 + 64 * (half // 2)
        pool[rows, 0:128] = one_hot(home4 == lane).astype(BF16)
        pool[rows, 128:256] = one_hot(home5 == lane).astype(BF16)
    three = one_hot(line % 16 == lane // 8).astype(BF16)
    fan[0:128, :] = three
    fan[128:256, :] = three
    fan[256:384, :] = one_hot(line % 8 == lane // 16).astype(BF16)
    fan[384:512, :] = one_hot(line % 4 == lane // 32).astype(BF16)


def kernel(nf, ns, rhs, dens, solution, residual, *scratch):
    scratch = list(scratch)

    def take(count):
        taken = scratch[:count]
        del scratch[:count]
        return taken

    refs = {}
    for name in ("D0", "D1", "D2", "R0", "R1", "R2"):
        (refs[name],) = take(1)
    fine_coef = [take(5) for _ in range(3)]
    remains = take(3)
    updates = [take(3) for _ in range(3)]
    answers = take(3)
    (work, tile_work, pair, sol, spread) = take(5)
    (spread_row, pool, fan, keep3, keep4, keep5) = take(6)
    coarse_coef = [take(5) for _ in range(3)]
    phases = []
    k, s = lax.axis_index("fine"), lax.axis_index("sub")
    for with_density in (True, False):
        count = n_halo(with_density)
        buffers = take(count), take(count), take(len(whole_messages(with_density)))
        coarse = take(4)
        send_sem, recv_sem = take(2)
        phases.append(
            Phase(refs, (k, s, nf, ns), with_density, buffers, coarse, send_sem, recv_sem)
        )
    ng = nf // ROW
    i, g = k % ROW, k // ROW

    barrier = pltpu.get_barrier_semaphore()
    partners = []
    for shift in (1, 2, 3):
        partners += [((k + shift) % nf, s), ((k + nf - shift) % nf, s)]
    partners += [(g * ROW + (i + delta) % ROW, s) for delta in range(1, ROW)]
    depth, side = partners_of((k, s, nf, ns))
    partners += depth + [device for _, device in side]
    for partner in partners:
        pl.semaphore_signal(barrier, inc=1, device_id=partner, device_id_type=MESH)

    pair[...] = jnp.zeros((16, 128), F32)

    def restrict_all(name, lead):
        for level in range(2):
            refs[name + str(level + 1)][
                lead : lead + PLANES[level + 1], 0 : ROWS[level + 1], :
            ] = restrict_block(
                refs[name + str(level)], lead, PLANES[level], ROWS[level], 2**level, work
            )

    def coefficients(level, low, high):
        fine_coefficients(level, refs["D" + str(level)], fine_coef[level], low, high)

    def smooth(level):
        fine_smooth(
            level,
            refs["R" + str(level)],
            fine_coef[level],
            remains[level],
            updates[level],
            answers[level],
        )

    line, lane = iota((128, 128), 0), iota((128, 128), 1)
    spread_row[...] = one_hot(line // 8 == lane % 16).astype(BF16)

    for cycle in range(CYCLES):
        phase = phases[cycle]
        if cycle == 0:
            phase.pack_row((rhs[...], dens[...]), pair, spread_row)
            pl.semaphore_wait(barrier, len(partners))
        else:
            phase.pack_row((refs["R0"][4:12, 0:32, :],), pair, spread_row)
        phase.start_rows()
        if cycle == 0:
            refs["R0"][4:12, 0:32, :] = rhs[...]
            refs["D0"][5:13, 0:32, :] = dens[...]
            restrict_all("D", 5)
        restrict_all("R", 4)
        phase.pack_x()
        phase.start_x()
        if cycle == 0:
            phase.start_whole({"D0": (dens, 0), "R0": (rhs, 0)})
        else:
            phase.start_whole({"R0": (refs["R0"], 4)})
        phase.pack_z("a")
        phase.start_z("a")
        if cycle == 0:
            build_matrices(pool, fan)
            for level in range(3):
                for name, lead in (("D", 5), ("R", 4)):
                    ref = refs[name + str(level)]
                    planes, rows, _ = ref.shape
                    blank = jnp.zeros((lead, rows, 128), F32)
                    ref[0:lead] = blank
                    ref[planes - lead : planes] = blank
            for ref in (keep4, keep5):
                rows = ref.shape[0]
                ref[0:8, :] = jnp.zeros((8, 128), F32)
                ref[rows - 8 : rows, :] = jnp.zeros((8, 128), F32)
        phase.start_depth()
        phase.unpack_x()
        phase.pack_z("b")
        phase.start_z("b")
        phase.start_sides(tile_work, pool)
        if cycle == 0:
            coefficients(0, 5, 11)
        else:
            phases[0].finish(0, None)
        phase.unpack_z()
        for level in (2, 1):
            if cycle == 0:
                coefficients(level, 0, PLANES[level] + 8)
            smooth(level)
        phase.unpack_whole()
        if cycle == 0:
            coefficients(0, 0, 5)
            coefficients(0, 11, 16)
        smooth(0)
        if cycle == 1:
            phase.finish(0, -7)
        phase.wait_sides()

        tiles = [phase.side_in[index % 8, index // 8] for index in range(ng)]
        line = iota((8, 128), 0)
        packed4, packed5 = [], []
        for index in range(0, ng, 2):
            packed4.append(jnp.where(line < 4, tiles[index], roll(tiles[index + 1], 4, 0)))
        for index in range(0, ng, 4):
            first = jnp.where(line < 6, tiles[index], tiles[index + 1])
            second = jnp.where(line < 6, tiles[index + 2], tiles[index + 3])
            packed5.append(jnp.where(line < 4, roll(first, 4, 0), second))
        source4, density4 = split_packed(jnp.concatenate(packed4, axis=0))
        source5, density5 = split_packed(jnp.concatenate(packed5, axis=0))
        if cycle == 0:
            low_in = jnp.where(g > 0, 1.0, 0.0).astype(F32)
            high_in = jnp.where(g < ng - 1, 1.0, 0.0).astype(F32)
            density3 = jnp.concatenate(
                [
                    phase.group_fields(g - 1)[1] * low_in,
                    phase.group_fields(g)[1],
                    phase.group_fields(g + 1)[1] * high_in,
                ],
                axis=0,
            )
            for index, (field, ny) in enumerate(
                ((density3, 16), (density4, 8), (density5, 4))
            ):
                values = packed_coefficients(field, ny, ny, 0.25 ** (3 + index))
                for ref, value in zip(coarse_coef[index], values):
                    ref[...] = value
        coef3, coef4, coef5 = ([ref[...] for ref in refs5] for refs5 in coarse_coef)
        total = jnp.sum(jnp.sum(source5, axis=0, keepdims=True), axis=1, keepdims=True)
        weight = jnp.sum(jnp.sum(coef5[3], axis=0, keepdims=True), axis=1, keepdims=True)
        n4, n5 = 4 * ng, 2 * ng
        keep5[8 : 8 + n5, :] = packed_smooth(source5, coef5, 4, 0.05) + total / weight
        keep4[8 : 8 + n4, :] = packed_smooth(source4, coef4, 8, 0.5)

        source3 = jnp.concatenate(
            [phase.group_fields(g + shift)[0] for shift in (-1, 0, 1)], axis=0
        )
        keep3[...] = packed_smooth(source3, coef3, 16, 0.5)

        row = iota((16, 512), 0)
        lane = iota((16, 512), 1)
        x3 = row // 2 + jnp.where(row < 12, 0, -8) + (4 * s + 4)
        inside = (x3 >= 4) & (x3 < 20)
        x_lane = jnp.where(
            lane < 256, lane // 16, jnp.where(lane < 384, (lane - 256) // 8, (lane - 384) // 4)
        )
        x_row = jnp.where(lane < 256, x3 - 4, jnp.where(lane < 384, x3 // 2 - 2, x3 // 4 - 1))
        chosen = (x_lane == x_row) & inside
        picked = []
        for t in range(3):
            parts = jnp.concatenate(
                [
                    keep3[pl.ds(7 + i + t, 1), :],
                    keep4[pl.ds((k + 1 + t) // 2 + 7, 1), :],
                    keep5[pl.ds((k + 3 + t) // 4 + 7, 1), :],
                ],
                axis=1,
            )
            picked.append(jnp.where(chosen, parts, 0.0))
        spread[0:3, 0:16, :] = one_hot_matmul(
            jnp.concatenate(picked, axis=0), fan[...]
        ).reshape(3, 16, 128)

        for level in (2, 1):
            rows = ROWS[level]
            answer = answers[level]
            planes = PLANES[level] + 2
            coarse = jnp.concatenate(
                [spread[(p + 1) // 2 : (p + 1) // 2 + 1, 0 : rows + 8, :] for p in range(planes)],
                axis=0,
            )
            value = answer[3 : 3 + planes] + coarse
            own, ends = value[:, 0:rows, :], value[:, rows : rows + 8, :]
            spread[0:planes, pl.ds(0, rows, stride=2), :] = own
            spread[0:planes, pl.ds(1, rows, stride=2), :] = own
            spread[0:planes, 2 * rows : 2 * rows + 8, :] = jnp.where(
                upper_rows(planes), ends[:, 0:1, :], ends[:, 7:8, :]
            )


        def advance(p, carry, cycle=cycle):
            step = 0.4 * (answers[0][p + 3] + spread[(p + 1) // 2])
            sol[p] = step if cycle == 0 else sol[p] + step
            return carry

        lax.fori_loop(0, PLANES[0] + 2, advance, 0, unroll=True)

        def defect(p, carry, cycle=cycle):
            applied = fine_apply(sol, p + 1, fine_coef[0], p + 4, 1)
            left = rhs[p] - applied[0:32, :]
            if cycle == 0:
                refs["R0"][p + 4, 0:32, :] = left
            else:
                residual[p] = left
                solution[p] = sol[p + 1, 0:32, :]
            return carry

        lax.fori_loop(0, PLANES[0], defect, 0, unroll=True)

    phases[1].finish(-7, None)


def scratch_shapes(ng):
    shapes = []
    for level in range(3):
        shapes.append(pltpu.VMEM((PLANES[level] + 10, ROWS[level] + 16, 128), F32))
    extents = [(PLANES[level] + 8, ROWS[level] + 8, 128) for level in range(3)]
    shapes += [pltpu.VMEM(extent, F32) for extent in extents]
    for extent in extents:
        shapes += [pltpu.VMEM(extent, F32)] * 5
    shapes += [pltpu.VMEM(extent, F32) for extent in extents]
    for extent in extents:
        shapes += [pltpu.VMEM(extent, F32)] * 3
    shapes += [pltpu.VMEM(extent, F32) for extent in extents]
    shapes += [
        pltpu.VMEM((4, 32, 128), F32),
        pltpu.VMEM((16, 128), F32),
        pltpu.VMEM((16, 128), F32),
        pltpu.VMEM((10, 40, 128), F32),
        pltpu.VMEM((6, 40, 128), F32),
        pltpu.VMEM((128, 128), BF16),
        pltpu.VMEM((512, 256), BF16),
        pltpu.VMEM((512, 128), BF16),
        pltpu.VMEM((24, 256), F32),
        pltpu.VMEM((4 * ng + 16, 128), F32),
        pltpu.VMEM((2 * ng + 16, 128), F32),
    ]
    for extent in ((24, 256), (4 * ng, 128), (2 * ng, 128)):
        shapes += [pltpu.VMEM(extent, F32)] * 5
    for with_density in (True, False):
        halo = buffer_shapes(with_density)
        shapes += halo + halo + whole_shapes(with_density)
        tiles = 10 if with_density else 6
        shapes += [
            pltpu.VMEM((1, 128), F32),
            pltpu.VMEM((ROW, 1, 128), F32),
            pltpu.VMEM((8, 8, 128), F32),
            pltpu.VMEM((8, tiles, 8, 128), F32),
        ]
        copies = n_halo(with_density) + len(whole_messages(with_density))
        copies += (ROW - 1) + 7 + 7
        shapes += [pltpu.SemaphoreType.DMA((copies,)), pltpu.SemaphoreType.DMA((copies,))]
    return shapes


def solution(mesh):
    nf, ns = mesh.shape["fine"], mesh.shape["sub"]

    def body(rhs, density):
        return pl.pallas_call(
            functools.partial(kernel, nf, ns),
            out_shape=(
                jax.ShapeDtypeStruct(rhs.shape, F32),
                jax.ShapeDtypeStruct(rhs.shape, F32),
            ),
            in_specs=[pl.BlockSpec(memory_space=pltpu.VMEM)] * 2,
            out_specs=[pl.BlockSpec(memory_space=pltpu.VMEM)] * 2,
            scratch_shapes=scratch_shapes(nf // ROW),
            compiler_params=pltpu.CompilerParams(
                collective_id=0, has_side_effects=True, vmem_limit_bytes=32 * 1024 * 1024
            ),
        )(rhs, density)

    return jax.shard_map(
        body,
        mesh=mesh,
        in_specs=(P("fine", "sub", None), P("fine", "sub", None)),
        out_specs=(P("fine", "sub", None), P("fine", "sub", None)),
        check_vma=False,
    )
```

profile of v0, /device:TPU:1, one launch (start us, length us, event | category | flops | bytes accessed | tf_op | source)
XLA Modules:
  0.0 49.3 jit_solution(14776747448899107742)
XLA Ops:
  0.6 0.0 copy-start
  0.6 0.9 %copy-done = f32[8,32,128]{2,1,0:T(8,128)S(1)} copy-done((f32[8,32,128]{2,1,0:T(8,128)S(1)}, f32[8,32,128]{2,1,0:T(8,128)}, u32[]{:S(2)}) %copy-start) | copy-done | bytes 131096
  1.5 0.0 copy-start.1
  1.5 0.9 %copy-done.1 = f32[8,32,128]{2,1,0:T(8,128)S(1)} copy-done((f32[8,32,128]{2,1,0:T(8,128)S(1)}, f32[8,32,128]{2,1,0:T(8,128)}, u32[]{:S(2)}) %copy-start.1) | copy-done | bytes 131096
  2.4 45.5 %shard_map.41 = (f32[8,32,128]{2,1,0:T(8,128)S(1)}, f32[8,32,128]{2,1,0:T(8,128)S(1)}) custom-call(f32[8,32,128]{2,1,0:T(8,128)S(1)} %copy-done, f32[8,32,128]{2,1,0:T(8,128)S(1)} %copy-done.1), custom_call_target="tpu_custom_call" | custom-call | tf_op jit(solution)/shard_map/pallas_call | solution.py:866
  48.0 0.7 %copy.6 = f32[8,32,128]{2,1,0:T(8,128)} copy(f32[8,32,128]{2,1,0:T(8,128)S(1)} %get-tuple-element.4) | data formatting | bytes 262144
  48.6 0.7 %copy.7 = f32[8,32,128]{2,1,0:T(8,128)} copy(f32[8,32,128]{2,1,0:T(8,128)S(1)} %get-tuple-element.5) | data formatting | bytes 262144
Async XLA Ops:
  0.6 0.9 %copy-start = (f32[8,32,128]{2,1,0:T(8,128)S(1)}, f32[8,32,128]{2,1,0:T(8,128)}, u32[]{:S(2)}) copy-start(f32[8,32,128]{2,1,0:T(8,128)} %rhs.1) | copy-start | bytes 393220
  1.5 0.9 %copy-start.1 = (f32[8,32,128]{2,1,0:T(8,128)S(1)}, f32[8,32,128]{2,1,0:T(8,128)}, u32[]{:S(2)}) copy-start(f32[8,32,128]{2,1,0:T(8,128)} %dens.1) | copy-start | bytes 393220
where the time goes:
time: 49.4 us; the launch traced here: 49.3 us
  Pallas kernels  45.5 us (92%)
  local copies, waits for them, and re-layouts  3.11 us (6%)
  between operations  0.65 us (1%)
    pallas_call x1, Pallas kernels, body(): pl.pallas_call(functools.partial(kernel, nf, ns), out_shape=(jax.ShapeDty...  45.5 us
    unnamed x6, local copies, waits for them, and re-layouts  3.11 us

commit v1 on v0

--- a/solution.py
+++ b/solution.py
@@ -211,36 +211,46 @@
 
 
 PIECES = {
-    ("a", 1): ((("D1", 5, 1, 4), ("D2", 5, 3, 2)), (("R1", 4, 0, 4), ("R2", 4, 2, 2))),
-    ("a", -1): ((("D1", 5, 9, 4), ("D2", 5, 7, 2)), (("R1", 4, 8, 4), ("R2", 4, 6, 2))),
-    ("a", 2): ((("D1", 8, 0, 1), ("D2", 5, 1, 2)), (("R2", 4, 0, 2),)),
-    ("a", -2): ((("D1", 5, 13, 1), ("D2", 5, 9, 2)), (("R2", 4, 8, 2),)),
-    ("a", 3): ((("D2", 6, 0, 1),), ()),
-    ("a", -3): ((("D2", 5, 11, 1),), ()),
-    ("b", 1): (
-        (("D0", 9, 1, 4), ("D1", 5, 1, 4), ("D2", 5, 3, 2)),
-        (("R0", 9, 1, 3), ("R1", 4, 0, 4), ("R2", 4, 2, 2)),
-    ),
-    ("b", -1): (
-        (("D0", 5, 13, 4), ("D1", 5, 9, 4), ("D2", 5, 7, 2)),
-        (("R0", 4, 12, 3), ("R1", 4, 8, 4), ("R2", 4, 6, 2)),
-    ),
-    ("b", 2): ((("D2", 5, 1, 2),), (("R2", 4, 0, 2),)),
-    ("b", -2): ((("D2", 5, 9, 2),), (("R2", 4, 8, 2),)),
+    ("first", 1): {
+        "a": (("D0", 8, 0, 5), ("R0", 8, 0, 4), ("D1", 5, 1, 4), ("D2", 5, 3, 2))
+        + (("R1", 4, 0, 4), ("R2", 4, 2, 2)),
+    },
+    ("first", -1): {
+        "a": (("D0", 5, 13, 5), ("R0", 4, 12, 4), ("D1", 5, 9, 4), ("D2", 5, 7, 2))
+        + (("R1", 4, 8, 4), ("R2", 4, 6, 2)),
+    },
+    ("first", 3): {"a": (("D2", 6, 0, 1),)},
+    ("first", -3): {"a": (("D2", 5, 11, 1),)},
+    ("second", 2): {
+        "a": (("D1", 8, 0, 1), ("D2", 5, 1, 2), ("R2", 4, 0, 2)),
+        "b": (("D2", 5, 1, 2), ("R2", 4, 0, 2)),
+    },
+    ("second", -2): {
+        "a": (("D1", 5, 13, 1), ("D2", 5, 9, 2), ("R2", 4, 8, 2)),
+        "b": (("D2", 5, 9, 2), ("R2", 4, 8, 2)),
+    },
+    ("second", 1): {
+        "b": (("D0", 9, 1, 4), ("D1", 5, 1, 4), ("D2", 5, 3, 2))
+        + (("R0", 9, 1, 3), ("R1", 4, 0, 4), ("R2", 4, 2, 2)),
+    },
+    ("second", -1): {
+        "b": (("D0", 5, 13, 4), ("D1", 5, 9, 4), ("D2", 5, 7, 2))
+        + (("R0", 4, 12, 3), ("R1", 4, 8, 4), ("R2", 4, 6, 2)),
+    },
 }
-WHOLE = (("D0", 1, 3, 0, 5), ("D0", -1, 0, 13, 5), ("R0", 1, 4, 0, 4), ("R0", -1, 0, 12, 4))
-
-
-def whole_messages(with_density):
-    return WHOLE if with_density else WHOLE[2:]
 
 
 def z_messages(with_density):
     result = []
-    for (part, shift), (density, field) in PIECES.items():
-        pieces = (density if with_density else ()) + field
+    for (stage, shift), parts in PIECES.items():
+        pieces = [
+            (part, piece)
+            for part, listed in parts.items()
+            for piece in listed
+            if with_density or piece[0][0] == "R"
+        ]
         if pieces:
-            result.append((part, shift, pieces))
+            result.append((stage, shift, pieces))
     return result
 
 
@@ -266,13 +276,9 @@
 
 def buffer_shapes(with_density):
     tiles = [sum(sent for _, _, sent in x_pieces(with_density))] * 2
-    for part, _, pieces in z_messages(with_density):
-        tiles.append(sum(piece_tiles(part, piece) for piece in pieces))
+    for _, _, pieces in z_messages(with_density):
+        tiles.append(sum(piece_tiles(part, piece) for part, piece in pieces))
     return [pltpu.VMEM((count, 8, 128), F32) for count in tiles]
-
-
-def whole_shapes(with_density):
-    return [pltpu.VMEM((count, 32, 128), F32) for _, _, _, _, count in whole_messages(with_density)]
 
 
 def n_halo(with_density):
@@ -313,9 +319,7 @@
 
 class Phase:
     def __init__(self, refs, place, with_density, buffers, coarse, send_sem, recv_sem):
-        send, recv, whole = buffers
-        self.whole_in = whole
-        self.whole = whole_messages(with_density)
+        send, recv = buffers
         self.refs = refs
         self.k, self.s, self.nf, self.ns = place
         self.dense = with_density
@@ -362,22 +366,27 @@
         else:
             pl.when(condition)(action)
 
-    def start_whole(self, fields):
-        self.whole_copies = []
-        for index, (name, shift, first, _, count) in enumerate(self.whole):
-            target = (self.k + shift + self.nf) % self.nf
-            ref, lead = fields[name]
-            source = ref.at[lead + first : lead + first + count, 0:32, :]
-            self.whole_copies.append(
-                self.start(source, self.whole_in[index], target, self.s, shift)
-            )
-
-    def unpack_whole(self):
-        for index, (name, shift, _, target, count) in enumerate(self.whole):
-            self.when(self.has_source(shift), self.whole_copies[index].wait_recv)
-        for index, (name, shift, _, target, count) in enumerate(self.whole):
-            block = jnp.where(self.has_source(shift), self.whole_in[index][...], 0.0)
-            self.refs[name][target : target + count, 0:32, :] = block
+    def start_all(self, pairs, total):
+        index = self.count
+        self.count += 1
+        sems = {"send_sem": self.send_sem.at[index], "recv_sem": self.recv_sem.at[index]}
+        for source, target, device in pairs:
+            pltpu.make_async_remote_copy(
+                src_ref=source,
+                dst_ref=target,
+                device_id=device,
+                device_id_type=MESH,
+                **sems,
+            ).start()
+        whole = pltpu.make_async_remote_copy(
+            src_ref=total,
+            dst_ref=total,
+            device_id=pairs[0][2],
+            device_id_type=MESH,
+            **sems,
+        )
+        self.started.append((whole, 0))
+        return whole
 
     def pack_x(self):
         for which in (0, 1):
@@ -434,12 +443,12 @@
                 block = unpack_lanes(block)
             ref[lead : lead + count, own : own + 8, :] = block
 
-    def pack_z(self, part):
-        for index, (kind, _, pieces) in enumerate(self.z):
-            if kind != part:
+    def pack_z(self, stage):
+        for index, (when, _, pieces) in enumerate(self.z):
+            if when != stage:
                 continue
             at = 0
-            for piece in pieces:
+            for part, piece in pieces:
                 name, source, _, count = piece
                 ref, own = self.refs[name], ROWS[int(name[1])]
                 if part == "a":
@@ -455,9 +464,9 @@
                 self.send[2 + index][at : at + block.shape[0]] = block
                 at += block.shape[0]
 
-    def start_z(self, part):
-        for index, (kind, shift, _) in enumerate(self.z):
-            if kind == part:
+    def start_z(self, stage):
+        for index, (when, shift, _) in enumerate(self.z):
+            if when == stage:
                 target = (self.k + shift + self.nf) % self.nf
                 self.copies[index] = self.start(
                     self.send[2 + index], self.recv[2 + index], target, self.s, shift
@@ -466,10 +475,10 @@
     def unpack_z(self):
         for index, (_, shift, _) in enumerate(self.z):
             self.when(self.has_source(shift), self.copies[index].wait_recv)
-        for index, (part, shift, pieces) in enumerate(self.z):
+        for index, (_, shift, pieces) in enumerate(self.z):
             inside = self.has_source(shift)
             at = 0
-            for piece in pieces:
+            for part, piece in pieces:
                 name, _, target, count = piece
                 ref, own = self.refs[name], ROWS[int(name[1])]
                 sent = piece_tiles(part, piece)
@@ -495,29 +504,24 @@
         self.row_in[self.i] = row
 
     def start_rows(self):
-        self.row_copies = []
-        for delta in range(1, ROW):
-            target = self.g * ROW + (self.i + delta) % ROW
-            self.row_copies.append(
-                self.start(self.row, self.row_in.at[self.i], target, self.s)
-            )
+        slot = self.row_in.at[self.i]
+        devices = [(self.g * ROW + (self.i + delta) % ROW, self.s) for delta in (4, 3, 5, 2, 6, 1, 7)]
+        pairs = [(self.row, slot, device) for device in devices]
+        self.row_copies = self.start_all(pairs, self.row_in.at[0 : ROW - 1])
 
     def start_depth(self):
-        for copy in self.row_copies:
-            copy.wait_recv()
+        self.row_copies.wait_recv()
         line = iota((8, 128), 0)
         tile = jnp.zeros((8, 128), F32)
         for index in range(ROW):
             tile = jnp.where(line == index, self.row_in[index], tile)
         self.depth_in[self.z_at] = tile
-        self.depth_copies = []
-        for k, s in self.depth_partners:
-            slot = self.depth_in.at[self.z_at]
-            self.depth_copies.append(self.start(slot, slot, k, s))
+        slot = self.depth_in.at[self.z_at]
+        pairs = [(slot, slot, device) for device in self.depth_partners]
+        self.depth_copies = self.start_all(pairs, self.depth_in.at[0:7])
 
     def start_sides(self, work, pool):
-        for copy in self.depth_copies:
-            copy.wait_recv()
+        self.depth_copies.wait_recv()
         left = iota((8, 128), 1) < 64
         slot = self.side_in.at[self.y]
         wide = []
@@ -542,13 +546,11 @@
             five = (five + roll(five, -2, 0)) * (0.125 * 0.125)
             five = jnp.where(line % 2 == 0, five[0:1], five[4:5])
             slot[half, 4:8, :] = five[4:8]
-        self.side_copies = []
-        for delta, (k, s) in self.side_partners:
-            if delta in (1, 7):
-                self.side_copies.append(self.start(slot, slot, k, s))
-            else:
-                part = slot.at[0:2]
-                self.side_copies.append(self.start(part, part, k, s))
+        part = slot.at[0:2]
+        far = [(part, part, device) for delta, device in self.side_partners if delta not in (1, 7)]
+        self.side_copies = [self.start_all(far, self.side_in.at[0:5, 0:2])]
+        near = [(slot, slot, device) for delta, device in self.side_partners if delta in (1, 7)]
+        self.side_copies.append(self.start_all(near, self.side_in.at[0:2]))
 
     def wait_sides(self):
         for copy in self.side_copies:
@@ -611,7 +613,7 @@
     k, s = lax.axis_index("fine"), lax.axis_index("sub")
     for with_density in (True, False):
         count = n_halo(with_density)
-        buffers = take(count), take(count), take(len(whole_messages(with_density)))
+        buffers = take(count), take(count)
         coarse = take(4)
         send_sem, recv_sem = take(2)
         phases.append(
@@ -671,12 +673,8 @@
         restrict_all("R", 4)
         phase.pack_x()
         phase.start_x()
-        if cycle == 0:
-            phase.start_whole({"D0": (dens, 0), "R0": (rhs, 0)})
-        else:
-            phase.start_whole({"R0": (refs["R0"], 4)})
-        phase.pack_z("a")
-        phase.start_z("a")
+        phase.pack_z("first")
+        phase.start_z("first")
         if cycle == 0:
             build_matrices(pool, fan)
             for level in range(3):
@@ -692,8 +690,8 @@
                 ref[rows - 8 : rows, :] = jnp.zeros((8, 128), F32)
         phase.start_depth()
         phase.unpack_x()
-        phase.pack_z("b")
-        phase.start_z("b")
+        phase.pack_z("second")
+        phase.start_z("second")
         phase.start_sides(tile_work, pool)
         if cycle == 0:
             coefficients(0, 5, 11)
@@ -704,13 +702,12 @@
             if cycle == 0:
                 coefficients(level, 0, PLANES[level] + 8)
             smooth(level)
-        phase.unpack_whole()
         if cycle == 0:
             coefficients(0, 0, 5)
             coefficients(0, 11, 16)
         smooth(0)
         if cycle == 1:
-            phase.finish(0, -7)
+            phase.finish(0, -2)
         phase.wait_sides()
 
         tiles = [phase.side_in[index % 8, index // 8] for index in range(ng)]
@@ -813,7 +810,7 @@
 
         lax.fori_loop(0, PLANES[0], defect, 0, unroll=True)
 
-    phases[1].finish(-7, None)
+    phases[1].finish(-2, None)
 
 
 def scratch_shapes(ng):
@@ -845,7 +842,7 @@
         shapes += [pltpu.VMEM(extent, F32)] * 5
     for with_density in (True, False):
         halo = buffer_shapes(with_density)
-        shapes += halo + halo + whole_shapes(with_density)
+        shapes += halo + halo
         tiles = 10 if with_density else 6
         shapes += [
             pltpu.VMEM((1, 128), F32),
@@ -853,8 +850,7 @@
             pltpu.VMEM((8, 8, 128), F32),
             pltpu.VMEM((8, tiles, 8, 128), F32),
         ]
-        copies = n_halo(with_density) + len(whole_messages(with_density))
-        copies += (ROW - 1) + 7 + 7
+        copies = n_halo(with_density) + 4
         shapes += [pltpu.SemaphoreType.DMA((copies,)), pltpu.SemaphoreType.DMA((copies,))]
     return shapes
 

time: 49.4 us -> 48.2 us (0.976)
  Pallas kernels: 45.5 us -> 44 us
    pallas_call x1, Pallas kernels: 45.5 us -> 44 us  [body(): pl.pallas_call(functools.partial(kernel, nf, ns), out_shape=(jax.ShapeDty...]
where the time goes in v1:
time: 48.2 us; the launch traced here: 47.8 us
  Pallas kernels  44 us (91%)
  local copies, waits for them, and re-layouts  3.11 us (6%)
  between operations  0.65 us (1%)
    pallas_call x1, Pallas kernels, body(): pl.pallas_call(functools.partial(kernel, nf, ns), out_shape=(jax.ShapeDty...  44 us
    unnamed x6, local copies, waits for them, and re-layouts  3.11 us

profile of v1, /device:TPU:1, one launch (start us, length us, event | category | flops | bytes accessed | tf_op | source)
XLA Modules:
  0.0 47.8 jit_solution(12643170290154972819)
XLA Ops:
  0.6 0.0 copy-start
  0.6 0.9 %copy-done = f32[8,32,128]{2,1,0:T(8,128)S(1)} copy-done((f32[8,32,128]{2,1,0:T(8,128)S(1)}, f32[8,32,128]{2,1,0:T(8,128)}, u32[]{:S(2)}) %copy-start) | copy-done | bytes 131096
  1.5 0.0 copy-start.1
  1.5 0.9 %copy-done.1 = f32[8,32,128]{2,1,0:T(8,128)S(1)} copy-done((f32[8,32,128]{2,1,0:T(8,128)S(1)}, f32[8,32,128]{2,1,0:T(8,128)}, u32[]{:S(2)}) %copy-start.1) | copy-done | bytes 131096
  2.4 44.0 %shard_map.41 = (f32[8,32,128]{2,1,0:T(8,128)S(1)}, f32[8,32,128]{2,1,0:T(8,128)S(1)}) custom-call(f32[8,32,128]{2,1,0:T(8,128)S(1)} %copy-done, f32[8,32,128]{2,1,0:T(8,128)S(1)} %copy-done.1), custom_call_target="tpu_custom_call" | custom-call | tf_op jit(solution)/shard_map/pallas_call | solution.py:862
  46.5 0.7 %copy.6 = f32[8,32,128]{2,1,0:T(8,128)} copy(f32[8,32,128]{2,1,0:T(8,128)S(1)} %get-tuple-element.4) | data formatting | bytes 262144
  47.1 0.7 %copy.7 = f32[8,32,128]{2,1,0:T(8,128)} copy(f32[8,32,128]{2,1,0:T(8,128)S(1)} %get-tuple-element.5) | data formatting | bytes 262144
Async XLA Ops:
  0.6 0.9 %copy-start = (f32[8,32,128]{2,1,0:T(8,128)S(1)}, f32[8,32,128]{2,1,0:T(8,128)}, u32[]{:S(2)}) copy-start(f32[8,32,128]{2,1,0:T(8,128)} %rhs.1) | copy-start | bytes 393220
  1.5 0.9 %copy-start.1 = (f32[8,32,128]{2,1,0:T(8,128)S(1)}, f32[8,32,128]{2,1,0:T(8,128)}, u32[]{:S(2)}) copy-start(f32[8,32,128]{2,1,0:T(8,128)} %dens.1) | copy-start | bytes 393220

commit v2 on v1

--- a/solution.py
+++ b/solution.py
@@ -35,6 +35,22 @@
     return lax.broadcasted_iota(jnp.int32, shape, dim)
 
 
+def div(value, divisor):
+    return value >> (divisor.bit_length() - 1)
+
+
+def mod(value, divisor):
+    return value & (divisor - 1)
+
+
+def quot(value, divisor):
+    return lax.div(value, jnp.int32(divisor))
+
+
+def rest(value, divisor):
+    return lax.rem(value, jnp.int32(divisor))
+
+
 def roll(value, shift, axis):
     return pltpu.roll(value, shift % value.shape[axis], axis)
 
@@ -67,7 +83,7 @@
         + work[0 : planes // 2, pl.ds(1, half, stride=2), :]
     )
     lane = iota(both.shape, 2)
-    even = (lane // stride) % 2 == 0
+    even = mod(div(lane, stride), 2) == 0
     other = jnp.where(even, roll(both, -stride, 2), roll(both, stride, 2))
     return (both + other) * 0.125
 
@@ -156,8 +172,8 @@
     rows = dens.shape[0]
     z = iota(dens.shape, 0)
     lane = iota(dens.shape, 1)
-    y = lane % ny
-    x = lane // ny
+    y = mod(lane, ny)
+    x = div(lane, ny)
     scale = 2.0 * scale
 
     def neighbour(shift, axis, outside):
@@ -286,7 +302,7 @@
 
 
 def even_lanes(tiles):
-    return iota((tiles, 8, 128), 2) % 2 == 0
+    return mod(iota((tiles, 8, 128), 2), 2) == 0
 
 
 def upper_rows(tiles):
@@ -308,12 +324,12 @@
 
 def partners_of(place):
     k, s, _, ns = place
-    i, y, half = k % ROW, k // ROW % 8, k // (8 * ROW)
+    i, y, half = rest(k, ROW), rest(quot(k, ROW), 8), quot(k, 8 * ROW)
     depth, side = [], []
     for delta in (4, 3, 5, 2, 6, 1, 7):
-        z = (half * ns + s + delta) % (2 * ns)
-        depth.append((((z // ns) * 8 + y) * ROW + i, z % ns))
-        side.append((delta, ((half * 8 + (y + delta) % 8) * ROW + i, s)))
+        z = rest(half * ns + s + delta, 2 * ns)
+        depth.append(((quot(z, ns) * 8 + y) * ROW + i, rest(z, ns)))
+        side.append((delta, ((half * 8 + rest(y + delta, 8)) * ROW + i, s)))
     return depth, side
 
 
@@ -330,11 +346,11 @@
         self.count = 0
         self.z = z_messages(with_density)
         self.copies = {}
-        self.i = self.k % ROW
-        self.g = self.k // ROW
+        self.i = rest(self.k, ROW)
+        self.g = quot(self.k, ROW)
         self.ng = self.nf // ROW
-        self.y = self.g % 8
-        self.z_at = self.g // 8 * self.ns + self.s
+        self.y = rest(self.g, 8)
+        self.z_at = quot(self.g, 8) * self.ns + self.s
         self.depth_partners, self.side_partners = partners_of(place)
 
     def start(self, source, target, k, s, shift=0):
@@ -409,7 +425,7 @@
                 at += sent
 
     def start_x(self):
-        up, down = (self.s + 1) % self.ns, (self.s + self.ns - 1) % self.ns
+        up, down = rest(self.s + 1, self.ns), rest(self.s + self.ns - 1, self.ns)
         self.x_copies = [
             self.start(self.send[0], self.recv[0], self.k, up),
             self.start(self.send[1], self.recv[1], self.k, down),
@@ -467,7 +483,7 @@
     def start_z(self, stage):
         for index, (when, shift, _) in enumerate(self.z):
             if when == stage:
-                target = (self.k + shift + self.nf) % self.nf
+                target = rest(self.k + shift + self.nf, self.nf)
                 self.copies[index] = self.start(
                     self.send[2 + index], self.recv[2 + index], target, self.s, shift
                 )
@@ -498,14 +514,16 @@
             pillar = jnp.sum(field, axis=0).reshape(4, 8, 128)
             pair[4 * index : 4 * index + 4, :] = jnp.sum(pillar, axis=1) * 0.125**3
         spread = one_hot_matmul(pair[...], spread_row[...])[0:8]
-        mine = iota((8, 128), 1) // 16 == iota((8, 128), 0)
+        mine = div(iota((8, 128), 1), 16) == iota((8, 128), 0)
         row = jnp.sum(jnp.where(mine, spread, 0.0), axis=0, keepdims=True)
         self.row[...] = row
         self.row_in[self.i] = row
 
     def start_rows(self):
         slot = self.row_in.at[self.i]
-        devices = [(self.g * ROW + (self.i + delta) % ROW, self.s) for delta in (4, 3, 5, 2, 6, 1, 7)]
+        devices = [
+            (self.g * ROW + rest(self.i + delta, ROW), self.s) for delta in (4, 3, 5, 2, 6, 1, 7)
+        ]
         pairs = [(self.row, slot, device) for device in devices]
         self.row_copies = self.start_all(pairs, self.row_in.at[0 : ROW - 1])
 
@@ -544,7 +562,7 @@
             five = sums[8 * half : 8 * half + 8, 128:256]
             five = five + roll(five, -1, 0)
             five = (five + roll(five, -2, 0)) * (0.125 * 0.125)
-            five = jnp.where(line % 2 == 0, five[0:1], five[4:5])
+            five = jnp.where(mod(line, 2) == 0, five[0:1], five[4:5])
             slot[half, 4:8, :] = five[4:8]
         part = slot.at[0:2]
         far = [(part, part, device) for delta, device in self.side_partners if delta not in (1, 7)]
@@ -557,8 +575,8 @@
             copy.wait_recv()
 
     def group_fields(self, group):
-        wrapped = (group + self.ng) % self.ng
-        y, half = wrapped % 8, wrapped // 8
+        wrapped = rest(group + self.ng, self.ng)
+        y, half = rest(wrapped, 8), quot(wrapped, 8)
         count = 4 if self.dense else 2
         tiles = [self.side_in[y, 2 + half * count + index] for index in range(count)]
         return [
@@ -578,17 +596,17 @@
 def build_matrices(pool, fan):
     line, lane = iota((128, 128), 0), iota((128, 128), 1)
     for half in range(4):
-        x, y = line // 16 + 8 * (half % 2), line % 16
+        x, y = div(line, 16) + 8 * (half % 2), mod(line, 16)
         rows = slice(128 * half, 128 * half + 128)
-        home4 = (x // 2) * 8 + y // 2 + 64 * (half // 2)
-        home5 = (x // 4) * 4 + y // 4 + 64 * (half // 2)
+        home4 = div(x, 2) * 8 + div(y, 2) + 64 * (half // 2)
+        home5 = div(x, 4) * 4 + div(y, 4) + 64 * (half // 2)
         pool[rows, 0:128] = one_hot(home4 == lane).astype(BF16)
         pool[rows, 128:256] = one_hot(home5 == lane).astype(BF16)
-    three = one_hot(line % 16 == lane // 8).astype(BF16)
+    three = one_hot(mod(line, 16) == div(lane, 8)).astype(BF16)
     fan[0:128, :] = three
     fan[128:256, :] = three
-    fan[256:384, :] = one_hot(line % 8 == lane // 16).astype(BF16)
-    fan[384:512, :] = one_hot(line % 4 == lane // 32).astype(BF16)
+    fan[256:384, :] = one_hot(mod(line, 8) == div(lane, 16)).astype(BF16)
+    fan[384:512, :] = one_hot(mod(line, 4) == div(lane, 32)).astype(BF16)
 
 
 def kernel(nf, ns, rhs, dens, solution, residual, *scratch):
@@ -620,13 +638,13 @@
             Phase(refs, (k, s, nf, ns), with_density, buffers, coarse, send_sem, recv_sem)
         )
     ng = nf // ROW
-    i, g = k % ROW, k // ROW
+    i, g = rest(k, ROW), quot(k, ROW)
 
     barrier = pltpu.get_barrier_semaphore()
     partners = []
     for shift in (1, 2, 3):
-        partners += [((k + shift) % nf, s), ((k + nf - shift) % nf, s)]
-    partners += [(g * ROW + (i + delta) % ROW, s) for delta in range(1, ROW)]
+        partners += [(rest(k + shift, nf), s), (rest(k + nf - shift, nf), s)]
+    partners += [(g * ROW + rest(i + delta, ROW), s) for delta in range(1, ROW)]
     depth, side = partners_of((k, s, nf, ns))
     partners += depth + [device for _, device in side]
     for partner in partners:
@@ -656,7 +674,7 @@
         )
 
     line, lane = iota((128, 128), 0), iota((128, 128), 1)
-    spread_row[...] = one_hot(line // 8 == lane % 16).astype(BF16)
+    spread_row[...] = one_hot(div(line, 8) == mod(lane, 16)).astype(BF16)
 
     for cycle in range(CYCLES):
         phase = phases[cycle]
@@ -675,6 +693,7 @@
         phase.start_x()
         phase.pack_z("first")
         phase.start_z("first")
+        phase.start_depth()
         if cycle == 0:
             build_matrices(pool, fan)
             for level in range(3):
@@ -688,7 +707,6 @@
                 rows = ref.shape[0]
                 ref[0:8, :] = jnp.zeros((8, 128), F32)
                 ref[rows - 8 : rows, :] = jnp.zeros((8, 128), F32)
-        phase.start_depth()
         phase.unpack_x()
         phase.pack_z("second")
         phase.start_z("second")
@@ -706,6 +724,29 @@
             coefficients(0, 0, 5)
             coefficients(0, 11, 16)
         smooth(0)
+
+        for level in (2, 1):
+            rows = ROWS[level]
+            planes = PLANES[level] + 2
+            value = answers[level][3 : 3 + planes]
+            if level == 1:
+                value = value + jnp.concatenate(
+                    [spread[(p + 1) // 2 : (p + 1) // 2 + 1, 0 : rows + 8, :] for p in range(planes)],
+                    axis=0,
+                )
+            own, ends = value[:, 0:rows, :], value[:, rows : rows + 8, :]
+            spread[0:planes, pl.ds(0, rows, stride=2), :] = own
+            spread[0:planes, pl.ds(1, rows, stride=2), :] = own
+            spread[0:planes, 2 * rows : 2 * rows + 8, :] = jnp.where(
+                upper_rows(planes), ends[:, 0:1, :], ends[:, 7:8, :]
+            )
+
+        def collect(p, carry, cycle=cycle):
+            step = 0.4 * (answers[0][p + 3] + spread[(p + 1) // 2])
+            sol[p] = step if cycle == 0 else sol[p] + step
+            return carry
+
+        lax.fori_loop(0, PLANES[0] + 2, collect, 0, unroll=True)
         if cycle == 1:
             phase.finish(0, -2)
         phase.wait_sides()
@@ -752,48 +793,39 @@
 
         row = iota((16, 512), 0)
         lane = iota((16, 512), 1)
-        x3 = row // 2 + jnp.where(row < 12, 0, -8) + (4 * s + 4)
+        x3 = div(row, 2) + jnp.where(row < 12, 0, -8) + (4 * s + 4)
         inside = (x3 >= 4) & (x3 < 20)
         x_lane = jnp.where(
-            lane < 256, lane // 16, jnp.where(lane < 384, (lane - 256) // 8, (lane - 384) // 4)
+            lane < 256,
+            div(lane, 16),
+            jnp.where(lane < 384, div(mod(lane, 128), 8), div(mod(lane, 128), 4)),
         )
-        x_row = jnp.where(lane < 256, x3 - 4, jnp.where(lane < 384, x3 // 2 - 2, x3 // 4 - 1))
+        x_row = jnp.where(lane < 256, x3 - 4, jnp.where(lane < 384, div(x3, 2) - 2, div(x3, 4) - 1))
         chosen = (x_lane == x_row) & inside
         picked = []
         for t in range(3):
             parts = jnp.concatenate(
                 [
                     keep3[pl.ds(7 + i + t, 1), :],
-                    keep4[pl.ds((k + 1 + t) // 2 + 7, 1), :],
-                    keep5[pl.ds((k + 3 + t) // 4 + 7, 1), :],
+                    keep4[pl.ds(quot(k + 1 + t, 2) + 7, 1), :],
+                    keep5[pl.ds(quot(k + 3 + t, 4) + 7, 1), :],
                 ],
                 axis=1,
             )
             picked.append(jnp.where(chosen, parts, 0.0))
-        spread[0:3, 0:16, :] = one_hot_matmul(
-            jnp.concatenate(picked, axis=0), fan[...]
-        ).reshape(3, 16, 128)
-
-        for level in (2, 1):
-            rows = ROWS[level]
-            answer = answers[level]
-            planes = PLANES[level] + 2
-            coarse = jnp.concatenate(
-                [spread[(p + 1) // 2 : (p + 1) // 2 + 1, 0 : rows + 8, :] for p in range(planes)],
-                axis=0,
+        lifted = one_hot_matmul(jnp.concatenate(picked, axis=0), fan[...]).reshape(3, 16, 128)
+
+        for t in range(3):
+            for tile in range(4):
+                spread[t, 8 * tile : 8 * tile + 8, :] = jnp.broadcast_to(
+                    lifted[t, 2 * tile : 2 * tile + 1, :], (8, 128)
+                )
+            spread[t, 32:40, :] = jnp.where(
+                iota((8, 128), 0) < 4, lifted[t, 8:9, :], lifted[t, 15:16, :]
             )
-            value = answer[3 : 3 + planes] + coarse
-            own, ends = value[:, 0:rows, :], value[:, rows : rows + 8, :]
-            spread[0:planes, pl.ds(0, rows, stride=2), :] = own
-            spread[0:planes, pl.ds(1, rows, stride=2), :] = own
-            spread[0:planes, 2 * rows : 2 * rows + 8, :] = jnp.where(
-                upper_rows(planes), ends[:, 0:1, :], ends[:, 7:8, :]
-            )
-
-
-        def advance(p, carry, cycle=cycle):
-            step = 0.4 * (answers[0][p + 3] + spread[(p + 1) // 2])
-            sol[p] = step if cycle == 0 else sol[p] + step
+
+        def advance(p, carry):
+            sol[p] = sol[p] + 0.4 * spread[(p + 7) // 8]
             return carry
 
         lax.fori_loop(0, PLANES[0] + 2, advance, 0, unroll=True)

time: 48.2 us -> 48.1 us (level)
  no operation moved by 1% of the time
where the time goes in v2:
time: 48.1 us; the launch traced here: 47.7 us
  Pallas kernels  43.9 us (91%)
  local copies, waits for them, and re-layouts  3.11 us (6%)
  between operations  0.65 us (1%)
    pallas_call x1, Pallas kernels, body(): pl.pallas_call(functools.partial(kernel, nf, ns), out_shape=(jax.ShapeDty...  43.9 us
    unnamed x6, local copies, waits for them, and re-layouts  3.11 us

profile of v2, /device:TPU:1, one launch (start us, length us, event | category | flops | bytes accessed | tf_op | source)
XLA Modules:
  0.0 47.7 jit_solution(16232727264377627971)
XLA Ops:
  0.6 0.0 copy-start
  0.6 0.9 %copy-done = f32[8,32,128]{2,1,0:T(8,128)S(1)} copy-done((f32[8,32,128]{2,1,0:T(8,128)S(1)}, f32[8,32,128]{2,1,0:T(8,128)}, u32[]{:S(2)}) %copy-start) | copy-done | bytes 131096
  1.5 0.0 copy-start.1
  1.5 0.9 %copy-done.1 = f32[8,32,128]{2,1,0:T(8,128)S(1)} copy-done((f32[8,32,128]{2,1,0:T(8,128)S(1)}, f32[8,32,128]{2,1,0:T(8,128)}, u32[]{:S(2)}) %copy-start.1) | copy-done | bytes 131096
  2.4 43.9 %shard_map.41 = (f32[8,32,128]{2,1,0:T(8,128)S(1)}, f32[8,32,128]{2,1,0:T(8,128)S(1)}) custom-call(f32[8,32,128]{2,1,0:T(8,128)S(1)} %copy-done, f32[8,32,128]{2,1,0:T(8,128)S(1)} %copy-done.1), custom_call_target="tpu_custom_call" | custom-call | tf_op jit(solution)/shard_map/pallas_call | solution.py:894
  46.4 0.7 %copy.6 = f32[8,32,128]{2,1,0:T(8,128)} copy(f32[8,32,128]{2,1,0:T(8,128)S(1)} %get-tuple-element.4) | data formatting | bytes 262144
  47.0 0.7 %copy.7 = f32[8,32,128]{2,1,0:T(8,128)} copy(f32[8,32,128]{2,1,0:T(8,128)S(1)} %get-tuple-element.5) | data formatting | bytes 262144
Async XLA Ops:
  0.6 0.9 %copy-start = (f32[8,32,128]{2,1,0:T(8,128)S(1)}, f32[8,32,128]{2,1,0:T(8,128)}, u32[]{:S(2)}) copy-start(f32[8,32,128]{2,1,0:T(8,128)} %rhs.1) | copy-start | bytes 393220
  1.5 0.9 %copy-start.1 = (f32[8,32,128]{2,1,0:T(8,128)S(1)}, f32[8,32,128]{2,1,0:T(8,128)}, u32[]{:S(2)}) copy-start(f32[8,32,128]{2,1,0:T(8,128)} %dens.1) | copy-start | bytes 393220

commit v3 on v2

--- a/solution.py
+++ b/solution.py
@@ -137,7 +137,7 @@
     return result
 
 
-def fine_smooth(level, source, coef, remain, updates, answer):
+def fine_smooth(level, source, coef, remain, updates, answer, inner, early):
     planes = PLANES[level] + 8
     stride = 2**level
     inverse = coef[4]
@@ -148,7 +148,15 @@
         d0[p] = source[p] * inverse[p] * first
         return carry
 
-    lax.fori_loop(0, planes, start, 0, unroll=True)
+    def planes_of(shrink):
+        low, high = shrink, planes - shrink
+        if inner is None:
+            return [(low, high)]
+        first_in, last_in = inner[0] + shrink, inner[1] - shrink
+        return [(first_in, last_in)] if early else [(low, first_in), (last_in, high)]
+
+    for low, high in planes_of(0):
+        lax.fori_loop(low, high, start, 0, unroll=True)
     chain = (d0, d1, d2)
     for sweep in range(3):
         old = chain[sweep]
@@ -165,7 +173,8 @@
                 answer[p] = d0[p] + d1[p] + d2[p] + new
             return carry
 
-        lax.fori_loop(sweep + 1, planes - sweep - 1, step, 0, unroll=True)
+        for low, high in planes_of(sweep + 1):
+            lax.fori_loop(low, high, step, 0, unroll=True)
 
 
 def packed_coefficients(dens, ny, nx, scale):
@@ -663,7 +672,7 @@
     def coefficients(level, low, high):
         fine_coefficients(level, refs["D" + str(level)], fine_coef[level], low, high)
 
-    def smooth(level):
+    def smooth(level, inner=None, early=False):
         fine_smooth(
             level,
             refs["R" + str(level)],
@@ -671,6 +680,8 @@
             remains[level],
             updates[level],
             answers[level],
+            inner,
+            early,
         )
 
     line, lane = iota((128, 128), 0), iota((128, 128), 1)
@@ -678,21 +689,25 @@
 
     for cycle in range(CYCLES):
         phase = phases[cycle]
-        if cycle == 0:
-            phase.pack_row((rhs[...], dens[...]), pair, spread_row)
-            pl.semaphore_wait(barrier, len(partners))
-        else:
-            phase.pack_row((refs["R0"][4:12, 0:32, :],), pair, spread_row)
-        phase.start_rows()
         if cycle == 0:
             refs["R0"][4:12, 0:32, :] = rhs[...]
             refs["D0"][5:13, 0:32, :] = dens[...]
             restrict_all("D", 5)
         restrict_all("R", 4)
         phase.pack_x()
+        if cycle == 0:
+            pl.semaphore_wait(barrier, len(partners))
         phase.start_x()
+        if cycle == 0:
+            phase.pack_row((rhs[...], dens[...]), pair, spread_row)
+        else:
+            phase.pack_row((refs["R0"][4:12, 0:32, :],), pair, spread_row)
+        phase.start_rows()
         phase.pack_z("first")
         phase.start_z("first")
+        phase.unpack_x()
+        phase.pack_z("second")
+        phase.start_z("second")
         phase.start_depth()
         if cycle == 0:
             build_matrices(pool, fan)
@@ -707,14 +722,13 @@
                 rows = ref.shape[0]
                 ref[0:8, :] = jnp.zeros((8, 128), F32)
                 ref[rows - 8 : rows, :] = jnp.zeros((8, 128), F32)
-        phase.unpack_x()
-        phase.pack_z("second")
-        phase.start_z("second")
         phase.start_sides(tile_work, pool)
+        inner = (5, 11) if cycle == 0 else (4, 12)
         if cycle == 0:
             coefficients(0, 5, 11)
         else:
             phases[0].finish(0, None)
+        smooth(0, inner, True)
         phase.unpack_z()
         for level in (2, 1):
             if cycle == 0:
@@ -723,7 +737,7 @@
         if cycle == 0:
             coefficients(0, 0, 5)
             coefficients(0, 11, 16)
-        smooth(0)
+        smooth(0, inner)
 
         for level in (2, 1):
             rows = ROWS[level]

time: 48.1 us -> 50.1 us (1.042)
  the two profiles are of different devices: /device:TPU:1 before, /device:TPU:8 now
where the time goes in v3:
time: 50.1 us; the launch traced here: 49.9 us
  Pallas kernels  46.2 us (92%)
  local copies, waits for them, and re-layouts  3.11 us (6%)
  between operations  0.65 us (1%)
    pallas_call x1, Pallas kernels, body(): pl.pallas_call(functools.partial(kernel, nf, ns), out_shape=(jax.ShapeDty...  46.2 us
    unnamed x6, local copies, waits for them, and re-layouts  3.11 us

profile of v3, /device:TPU:8, one launch (start us, length us, event | category | flops | bytes accessed | tf_op | source)
XLA Modules:
  0.0 49.9 jit_solution(12702913116262968441)
XLA Ops:
  0.6 0.0 copy-start
  0.6 0.9 %copy-done = f32[8,32,128]{2,1,0:T(8,128)S(1)} copy-done((f32[8,32,128]{2,1,0:T(8,128)S(1)}, f32[8,32,128]{2,1,0:T(8,128)}, u32[]{:S(2)}) %copy-start) | copy-done | bytes 131096
  1.5 0.0 copy-start.1
  1.5 0.9 %copy-done.1 = f32[8,32,128]{2,1,0:T(8,128)S(1)} copy-done((f32[8,32,128]{2,1,0:T(8,128)S(1)}, f32[8,32,128]{2,1,0:T(8,128)}, u32[]{:S(2)}) %copy-start.1) | copy-done | bytes 131096
  2.4 46.2 %shard_map.41 = (f32[8,32,128]{2,1,0:T(8,128)S(1)}, f32[8,32,128]{2,1,0:T(8,128)S(1)}) custom-call(f32[8,32,128]{2,1,0:T(8,128)S(1)} %copy-done, f32[8,32,128]{2,1,0:T(8,128)S(1)} %copy-done.1), custom_call_target="tpu_custom_call" | custom-call | tf_op jit(solution)/shard_map/pallas_call | solution.py:908
  48.6 0.7 %copy.6 = f32[8,32,128]{2,1,0:T(8,128)} copy(f32[8,32,128]{2,1,0:T(8,128)S(1)} %get-tuple-element.4) | data formatting | bytes 262144
  49.3 0.7 %copy.7 = f32[8,32,128]{2,1,0:T(8,128)} copy(f32[8,32,128]{2,1,0:T(8,128)S(1)} %get-tuple-element.5) | data formatting | bytes 262144
Async XLA Ops:
  0.6 0.9 %copy-start = (f32[8,32,128]{2,1,0:T(8,128)S(1)}, f32[8,32,128]{2,1,0:T(8,128)}, u32[]{:S(2)}) copy-start(f32[8,32,128]{2,1,0:T(8,128)} %rhs.1) | copy-start | bytes 393220
  1.5 0.9 %copy-start.1 = (f32[8,32,128]{2,1,0:T(8,128)S(1)}, f32[8,32,128]{2,1,0:T(8,128)}, u32[]{:S(2)}) copy-start(f32[8,32,128]{2,1,0:T(8,128)} %dens.1) | copy-start | bytes 393220

commit v4 on v3

--- a/solution.py
+++ b/solution.py
@@ -690,24 +690,20 @@
     for cycle in range(CYCLES):
         phase = phases[cycle]
         if cycle == 0:
+            phase.pack_row((rhs[...], dens[...]), pair, spread_row)
+            pl.semaphore_wait(barrier, len(partners))
+        else:
+            phase.pack_row((refs["R0"][4:12, 0:32, :],), pair, spread_row)
+        phase.start_rows()
+        if cycle == 0:
             refs["R0"][4:12, 0:32, :] = rhs[...]
             refs["D0"][5:13, 0:32, :] = dens[...]
             restrict_all("D", 5)
         restrict_all("R", 4)
         phase.pack_x()
-        if cycle == 0:
-            pl.semaphore_wait(barrier, len(partners))
         phase.start_x()
-        if cycle == 0:
-            phase.pack_row((rhs[...], dens[...]), pair, spread_row)
-        else:
-            phase.pack_row((refs["R0"][4:12, 0:32, :],), pair, spread_row)
-        phase.start_rows()
         phase.pack_z("first")
         phase.start_z("first")
-        phase.unpack_x()
-        phase.pack_z("second")
-        phase.start_z("second")
         phase.start_depth()
         if cycle == 0:
             build_matrices(pool, fan)
@@ -722,6 +718,9 @@
                 rows = ref.shape[0]
                 ref[0:8, :] = jnp.zeros((8, 128), F32)
                 ref[rows - 8 : rows, :] = jnp.zeros((8, 128), F32)
+        phase.unpack_x()
+        phase.pack_z("second")
+        phase.start_z("second")
         phase.start_sides(tile_work, pool)
         inner = (5, 11) if cycle == 0 else (4, 12)
         if cycle == 0:

time: 50.1 us -> 48.1 us (0.960)
  the two profiles are of different devices: /device:TPU:8 before, /device:TPU:1 now
where the time goes in v4:
time: 48.1 us; the launch traced here: 47.7 us
  Pallas kernels  43.9 us (91%)
  local copies, waits for them, and re-layouts  3.11 us (6%)
  between operations  0.65 us (1%)
    pallas_call x1, Pallas kernels, body(): pl.pallas_call(functools.partial(kernel, nf, ns), out_shape=(jax.ShapeDty...  43.9 us
    unnamed x6, local copies, waits for them, and re-layouts  3.11 us

profile of v4, /device:TPU:1, one launch (start us, length us, event | category | flops | bytes accessed | tf_op | source)
XLA Modules:
  0.0 47.7 jit_solution(10397809799228784191)
XLA Ops:
  0.6 0.0 copy-start
  0.6 0.9 %copy-done = f32[8,32,128]{2,1,0:T(8,128)S(1)} copy-done((f32[8,32,128]{2,1,0:T(8,128)S(1)}, f32[8,32,128]{2,1,0:T(8,128)}, u32[]{:S(2)}) %copy-start) | copy-done | bytes 131096
  1.5 0.0 copy-start.1
  1.5 0.9 %copy-done.1 = f32[8,32,128]{2,1,0:T(8,128)S(1)} copy-done((f32[8,32,128]{2,1,0:T(8,128)S(1)}, f32[8,32,128]{2,1,0:T(8,128)}, u32[]{:S(2)}) %copy-start.1) | copy-done | bytes 131096
  2.4 43.9 %shard_map.41 = (f32[8,32,128]{2,1,0:T(8,128)S(1)}, f32[8,32,128]{2,1,0:T(8,128)S(1)}) custom-call(f32[8,32,128]{2,1,0:T(8,128)S(1)} %copy-done, f32[8,32,128]{2,1,0:T(8,128)S(1)} %copy-done.1), custom_call_target="tpu_custom_call" | custom-call | tf_op jit(solution)/shard_map/pallas_call | solution.py:907
  46.4 0.7 %copy.6 = f32[8,32,128]{2,1,0:T(8,128)} copy(f32[8,32,128]{2,1,0:T(8,128)S(1)} %get-tuple-element.4) | data formatting | bytes 262144
  47.0 0.7 %copy.7 = f32[8,32,128]{2,1,0:T(8,128)} copy(f32[8,32,128]{2,1,0:T(8,128)S(1)} %get-tuple-element.5) | data formatting | bytes 262144
Async XLA Ops:
  0.6 0.9 %copy-start = (f32[8,32,128]{2,1,0:T(8,128)S(1)}, f32[8,32,128]{2,1,0:T(8,128)}, u32[]{:S(2)}) copy-start(f32[8,32,128]{2,1,0:T(8,128)} %rhs.1) | copy-start | bytes 393220
  1.5 0.9 %copy-start.1 = (f32[8,32,128]{2,1,0:T(8,128)S(1)}, f32[8,32,128]{2,1,0:T(8,128)}, u32[]{:S(2)}) copy-start(f32[8,32,128]{2,1,0:T(8,128)} %dens.1) | copy-start | bytes 393220

commit v5 on v4

--- a/solution.py
+++ b/solution.py
@@ -718,10 +718,10 @@
                 rows = ref.shape[0]
                 ref[0:8, :] = jnp.zeros((8, 128), F32)
                 ref[rows - 8 : rows, :] = jnp.zeros((8, 128), F32)
+        phase.start_sides(tile_work, pool)
         phase.unpack_x()
         phase.pack_z("second")
         phase.start_z("second")
-        phase.start_sides(tile_work, pool)
         inner = (5, 11) if cycle == 0 else (4, 12)
         if cycle == 0:
             coefficients(0, 5, 11)

time: 48.1 us -> 50.2 us (1.044)
  Pallas kernels: 43.9 us -> 46.1 us
    pallas_call x1, Pallas kernels: 43.9 us -> 46.1 us  [body(): pl.pallas_call(functools.partial(kernel, nf, ns), out_shape=(jax.ShapeDty...]
where the time goes in v5:
time: 50.2 us; the launch traced here: 49.8 us
  Pallas kernels  46.1 us (92%)
  local copies, waits for them, and re-layouts  3.11 us (6%)
  between operations  0.65 us (1%)
    pallas_call x1, Pallas kernels, body(): pl.pallas_call(functools.partial(kernel, nf, ns), out_shape=(jax.ShapeDty...  46.1 us
    unnamed x6, local copies, waits for them, and re-layouts  3.11 us

profile of v5, /device:TPU:1, one launch (start us, length us, event | category | flops | bytes accessed | tf_op | source)
XLA Modules:
  0.0 49.8 jit_solution(8209211174068712126)
XLA Ops:
  0.6 0.0 copy-start
  0.6 0.9 %copy-done = f32[8,32,128]{2,1,0:T(8,128)S(1)} copy-done((f32[8,32,128]{2,1,0:T(8,128)S(1)}, f32[8,32,128]{2,1,0:T(8,128)}, u32[]{:S(2)}) %copy-start) | copy-done | bytes 131096
  1.5 0.0 copy-start.1
  1.5 0.9 %copy-done.1 = f32[8,32,128]{2,1,0:T(8,128)S(1)} copy-done((f32[8,32,128]{2,1,0:T(8,128)S(1)}, f32[8,32,128]{2,1,0:T(8,128)}, u32[]{:S(2)}) %copy-start.1) | copy-done | bytes 131096
  2.4 46.1 %shard_map.41 = (f32[8,32,128]{2,1,0:T(8,128)S(1)}, f32[8,32,128]{2,1,0:T(8,128)S(1)}) custom-call(f32[8,32,128]{2,1,0:T(8,128)S(1)} %copy-done, f32[8,32,128]{2,1,0:T(8,128)S(1)} %copy-done.1), custom_call_target="tpu_custom_call" | custom-call | tf_op jit(solution)/shard_map/pallas_call | solution.py:907
  48.5 0.7 %copy.6 = f32[8,32,128]{2,1,0:T(8,128)} copy(f32[8,32,128]{2,1,0:T(8,128)S(1)} %get-tuple-element.4) | data formatting | bytes 262144
  49.2 0.7 %copy.7 = f32[8,32,128]{2,1,0:T(8,128)} copy(f32[8,32,128]{2,1,0:T(8,128)S(1)} %get-tuple-element.5) | data formatting | bytes 262144
Async XLA Ops:
  0.6 0.9 %copy-start = (f32[8,32,128]{2,1,0:T(8,128)S(1)}, f32[8,32,128]{2,1,0:T(8,128)}, u32[]{:S(2)}) copy-start(f32[8,32,128]{2,1,0:T(8,128)} %rhs.1) | copy-start | bytes 393220
  1.5 0.9 %copy-start.1 = (f32[8,32,128]{2,1,0:T(8,128)S(1)}, f32[8,32,128]{2,1,0:T(8,128)}, u32[]{:S(2)}) copy-start(f32[8,32,128]{2,1,0:T(8,128)} %dens.1) | copy-start | bytes 393220
